TPU v7x, 32 devices: a whole 2x2x4 slice. The times are simulated.
32 devices in a mesh: dp: 4 (over y, core), ctx: 8 (over z, x).
Axes of the slice: x: 2, y: 2, z: 4, core: 2. Of those that a mesh axis runs over, the one named last changes fastest.
Arguments:
- layer_input: bfloat16 [2, 4, 1024, 768], P(None, 'dp', 'ctx'), may hold values from -6 to 6
- doc_lengths: int32 [2, 4, 5], P(None, 'dp'), may hold values from 1 to 1020, as said below
- ln1_gain: float32 [768], replicated, may hold values from 0.5 to 1.5
- ln1_bias: float32 [768], replicated, may hold values from -3 to 3
- w_qkv: bfloat16 [768, 2304], P('dp'), may hold values from -0.21875 to 0.21875
- w_out: bfloat16 [768, 768], P('dp'), may hold values from -1.25 to 1.25
- ln2_gain: float32 [768], replicated, may hold values from 0.5 to 1.5
- ln2_bias: float32 [768], replicated, may hold values from -3 to 3
- w_up: bfloat16 [768, 3072], P('dp'), may hold values from -0.21875 to 0.21875
- b_up: float32 [3072], replicated, may hold values from -3 to 3
- w_down: bfloat16 [3072, 768], P('dp'), may hold values from -0.109375 to 0.109375
- cotangent: bfloat16 [2, 4, 1024, 768], P(None, 'dp', 'ctx'), may hold values from -6 to 6
Outputs:
- layer_output: bfloat16 [2, 4, 1024, 768], P(None, 'dp', 'ctx')
- d_x: bfloat16 [2, 4, 1024, 768], P(None, 'dp', 'ctx')
- d_ln1_gain: float32 [768], replicated
- d_ln1_bias: float32 [768], replicated
- d_w_qkv: float32 [768, 2304], P('dp', 'ctx')
- d_w_out: float32 [768, 768], P('dp', 'ctx')
- d_ln2_gain: float32 [768], replicated
- d_ln2_bias: float32 [768], replicated
- d_w_up: float32 [768, 3072], P('dp', 'ctx')
- d_b_up: float32 [3072], replicated
- d_w_down: float32 [3072, 768], P('dp', 'ctx')
Inputs may be any that keep to these rules, and one draw needn't show every extreme that they name: `doc_lengths`: each row packs 5 documents in order: a first one shorter than 128 tokens, a second one that ends within the last 128 positions of the row, then 5 - 2 documents of at most 32 tokens each; positions after their sum are padding. Some row of each draw has padding of zero length.
All inputs are finite; a program needn't handle non-finite values.
Results may differ from a plain program's by a relative error of at most 0.014.
Values may be sent and summed in bfloat16 or wider, within the bound.
A program may use at most 256 MiB of HBM per device.

v0:
```python
from functools import partial

import jax
import jax.numpy as jnp
from jax import lax
from jax.sharding import PartitionSpec as P

HD = 64


NORM_EPSILON = 1e-05
MASKED = -1e30
START_TOP = -1e20


def prefix_2(array, axis, combine, identity, reverse):
    peers, index = (lax.axis_size(axis), lax.axis_index(axis))
    everything = lax.all_gather(array, axis)
    start = jnp.broadcast_to(jnp.asarray(identity, array.dtype), array.shape)

    def turn(k, before):
        at = peers - 1 - k if reverse else k
        reached = at > index if reverse else at < index
        new = combine(before, everything[at])
        return jnp.where(reached, new, before)

    return lax.fori_loop(0, peers, turn, start)


def layer_norm(value, gain, bias):
    row_mean = jnp.mean(value, axis=-1, keepdims=True)
    centered = value - row_mean
    spread = jnp.mean(centered * centered, axis=-1, keepdims=True)
    return centered * lax.rsqrt(spread + NORM_EPSILON) * gain + bias


def matmul(left, right):
    return jnp.dot(left, right, preferred_element_type=jnp.float32)


def contract_rows(left, right):
    return lax.dot_general(
        left, right, (((0,), (0,)), ((), ())), preferred_element_type=jnp.float32
    )


def contract_cols(left, right):
    return lax.dot_general(
        left, right, (((1,), (1,)), ((), ())), preferred_element_type=jnp.float32
    )


def segment_table(lengths, row_length):
    doc_ends = jnp.cumsum(lengths)
    places = jnp.arange(row_length, dtype=jnp.int32)
    segment = jnp.sum((places[:, None] >= doc_ends[None, :]).astype(jnp.int32), axis=1)
    opening = jnp.concatenate([jnp.ones((1,), jnp.bool_), segment[1:] != segment[:-1]])
    return (segment, opening)


def add_up(earlier, later):
    return earlier + later


def on_device(
    layer_input,
    doc_lengths,
    ln1_gain,
    ln1_bias,
    w_qkv,
    w_out,
    ln2_gain,
    ln2_bias,
    w_up,
    b_up,
    w_down,
    cotangent,
):
    micro_count = layer_input.shape[0]
    query_rows = layer_input.shape[2]
    model_width = layer_input.shape[3]
    head_count = model_width // HD
    row_length = query_rows * lax.axis_size("ctx")
    key_block = min(512, row_length)
    score_scale = HD ** (-0.5)
    strength = 8.0 / row_length
    ctx_place = lax.axis_index("ctx")
    query_pos = ctx_place * query_rows + jnp.arange(query_rows, dtype=jnp.int32)
    block_total = ((ctx_place + 1) * query_rows + key_block - 1) // key_block
    later_heads = (jnp.arange(head_count) > 0).astype(jnp.float32)[:, None, None]
    zeros_row = jnp.zeros((row_length,), jnp.float32)
    gelu_exact = partial(jax.nn.gelu, approximate=False)
    output_list = []
    input_grads = []
    matrix_total = None
    vector_total = None
    for micro_step in range(micro_count):
        w_qkv_all, w_out_all, w_up_all, w_down_all = (
            lax.all_gather(w_qkv, "dp", axis=0, tiled=True),
            lax.all_gather(w_out, "dp", axis=0, tiled=True),
            lax.all_gather(w_up, "dp", axis=0, tiled=True),
            lax.all_gather(w_down, "dp", axis=0, tiled=True),
        )
        inputs = layer_input[micro_step, 0].astype(jnp.float32)
        segment, opening = segment_table(doc_lengths[micro_step, 0], row_length)
        query_seg = lax.dynamic_slice_in_dim(segment, ctx_place * query_rows, query_rows, 0)
        normed_one = layer_norm(inputs, ln1_gain, ln1_bias).astype(jnp.bfloat16)
        projected = matmul(normed_one, w_qkv_all).astype(jnp.bfloat16)
        queries = projected[:, :model_width]
        queries3 = queries.reshape(query_rows, head_count, HD)
        query_zero = queries[:, :HD]
        keys_all, values_all = (
            lax.all_gather(projected[:, model_width : 2 * model_width], "ctx", axis=0, tiled=True),
            lax.all_gather(projected[:, 2 * model_width :], "ctx", axis=0, tiled=True),
        )

        def masks(key_start):
            key_seg = lax.dynamic_slice_in_dim(segment, key_start, key_block, 0)
            key_open = lax.dynamic_slice_in_dim(opening, key_start, key_block, 0)
            key_pos = key_start + jnp.arange(key_block, dtype=jnp.int32)
            same_doc = query_seg[:, None] == key_seg[None, :]
            allowed = same_doc & (key_pos[None, :] <= query_pos[:, None])
            chosen = (
                same_doc
                & (key_pos[None, :] < query_pos[:, None])
                & jnp.logical_not(key_open)[None, :]
            )
            return (allowed, chosen.astype(jnp.float32))

        def head_scores(key_start):
            key_zero = lax.dynamic_slice_in_dim(keys_all, key_start, key_block, 0)[:, :HD]
            return (key_zero, contract_cols(query_zero, key_zero) * score_scale)

        def block_keys(key_start):
            keys3 = lax.dynamic_slice_in_dim(keys_all, key_start, key_block, 0).reshape(
                key_block, head_count, HD
            )
            values3 = lax.dynamic_slice_in_dim(values_all, key_start, key_block, 0).reshape(
                key_block, head_count, HD
            )
            return (keys3, values3)

        def logits_of(key_start, keys3):
            allowed, chosen = masks(key_start)
            raw_scores = (
                jnp.einsum("qhd,khd->hqk", queries3, keys3, preferred_element_type=jnp.float32)
                * score_scale
            )
            picked = strength * jax.nn.softplus(raw_scores[0]) * chosen
            before = lax.dynamic_slice_in_dim(prefix, key_start, key_block, 0)
            penalty = before[None, :] + jnp.cumsum(picked, axis=0) - picked
            return jnp.where(allowed[None], raw_scores - penalty[None], MASKED)

        def total_block(block_index, totals):
            key_start = block_index * key_block
            _, chosen = masks(key_start)
            _, first_scores = head_scores(key_start)
            picked = strength * jax.nn.softplus(first_scores) * chosen
            return lax.dynamic_update_slice_in_dim(totals, jnp.sum(picked, axis=0), key_start, 0)

        totals = lax.fori_loop(0, block_total, total_block, zeros_row)
        prefix = prefix_2(totals, "ctx", add_up, zeros_row, False)

        def stat_block(block_index, running):
            row_top, row_total = running
            key_start = block_index * key_block
            keys3, _ = block_keys(key_start)
            logits = logits_of(key_start, keys3)
            new_top = jnp.maximum(row_top, jnp.max(logits, axis=-1))
            row_total = row_total * jnp.exp(row_top - new_top) + jnp.sum(
                jnp.exp(logits - new_top[..., None]), axis=-1
            )
            return (new_top, row_total)

        row_top, row_total = lax.fori_loop(
            0,
            block_total,
            stat_block,
            (
                jnp.full((head_count, query_rows), START_TOP, jnp.float32),
                jnp.zeros((head_count, query_rows), jnp.float32),
            ),
        )
        log_total = row_top + jnp.log(row_total)

        def out_block(block_index, gathered_out):
            key_start = block_index * key_block
            keys3, values3 = block_keys(key_start)
            attn_probs = jnp.exp(logits_of(key_start, keys3) - log_total[..., None]).astype(
                jnp.bfloat16
            )
            return gathered_out + jnp.einsum(
                "hqk,khd->qhd", attn_probs, values3, preferred_element_type=jnp.float32
            )

        gathered_out = lax.fori_loop(
            0, block_total, out_block, jnp.zeros((query_rows, head_count, HD), jnp.float32)
        )
        attended = gathered_out.reshape(query_rows, model_width).astype(jnp.bfloat16)
        mid_stream = inputs + matmul(attended, w_out_all)
        normed_two = layer_norm(mid_stream, ln2_gain, ln2_bias).astype(jnp.bfloat16)
        hidden = matmul(normed_two, w_up_all) + b_up
        activated = gelu_exact(hidden).astype(jnp.bfloat16)
        output_list.append((mid_stream + matmul(activated, w_down_all)).astype(jnp.bfloat16))
        cot_rows = cotangent[micro_step, 0]
        grad_down = contract_rows(activated, cot_rows)
        grad_act = contract_cols(cot_rows, w_down_all)
        _, gelu_back = jax.vjp(gelu_exact, hidden)
        grad_hidden = gelu_back(grad_act)[0].astype(jnp.bfloat16)
        grad_up = contract_rows(normed_two, grad_hidden)
        grad_bias_up = jnp.sum(grad_hidden.astype(jnp.float32), axis=0)
        grad_normed_two = contract_cols(grad_hidden, w_up_all)
        _, norm_two_back = jax.vjp(layer_norm, mid_stream, ln2_gain, ln2_bias)
        grad_mid_part, grad_gain_two, grad_bias_two = norm_two_back(grad_normed_two)
        grad_mid = cot_rows.astype(jnp.float32) + grad_mid_part
        grad_branch = grad_mid.astype(jnp.bfloat16)
        grad_outproj = contract_rows(attended, grad_branch)
        grad_attended = contract_cols(grad_branch, w_out_all).astype(jnp.bfloat16)
        grad_att3 = grad_attended.reshape(query_rows, head_count, HD)
        row_delta = jnp.einsum("qhd,qhd->hq", grad_att3.astype(jnp.float32), gathered_out)

        def grad_block(block_index, running):
            grad_query, grad_key_all, grad_value_all, penalty_grad, first_grad = running
            key_start = block_index * key_block
            keys3, values3 = block_keys(key_start)
            probs_f32 = jnp.exp(logits_of(key_start, keys3) - log_total[..., None])
            grad_probs = jnp.einsum(
                "qhd,khd->hqk", grad_att3, values3, preferred_element_type=jnp.float32
            )
            grad_logits = probs_f32 * (grad_probs - row_delta[..., None])
            penalty_grad = lax.dynamic_update_slice_in_dim(
                penalty_grad, -jnp.sum(grad_logits, axis=0), key_start, 1
            )
            first_grad = lax.dynamic_update_slice_in_dim(first_grad, grad_logits[0], key_start, 1)
            grad_scores = (grad_logits * later_heads).astype(jnp.bfloat16)
            grad_query = (
                grad_query
                + jnp.einsum("hqk,khd->qhd", grad_scores, keys3, preferred_element_type=jnp.float32)
                * score_scale
            )
            key_part = (
                jnp.einsum(
                    "hqk,qhd->khd", grad_scores, queries3, preferred_element_type=jnp.float32
                )
                * score_scale
            )
            value_part = jnp.einsum(
                "hqk,qhd->khd",
                probs_f32.astype(jnp.bfloat16),
                grad_att3,
                preferred_element_type=jnp.float32,
            )
            grad_key_all = lax.dynamic_update_slice_in_dim(
                grad_key_all, key_part.reshape(key_block, model_width), key_start, 0
            )
            grad_value_all = lax.dynamic_update_slice_in_dim(
                grad_value_all, value_part.reshape(key_block, model_width), key_start, 0
            )
            return (grad_query, grad_key_all, grad_value_all, penalty_grad, first_grad)

        grad_query, grad_key_all, grad_value_all, penalty_grad, first_grad = lax.fori_loop(
            0,
            block_total,
            grad_block,
            (
                jnp.zeros((query_rows, head_count, HD), jnp.float32),
                jnp.zeros((row_length, model_width), jnp.float32),
                jnp.zeros((row_length, model_width), jnp.float32),
                jnp.zeros((query_rows, row_length), jnp.float32),
                jnp.zeros((query_rows, row_length), jnp.float32),
            ),
        )
        column_sums = jnp.sum(penalty_grad, axis=0)
        after = prefix_2(column_sums, "ctx", add_up, zeros_row, True)
        reach_sums = after + column_sums

        def head_block(block_index, running):
            grad_query_zero, grad_key_all = running
            key_start = block_index * key_block
            _, chosen = masks(key_start)
            key_zero, first_scores = head_scores(key_start)
            flow_block = lax.dynamic_slice_in_dim(penalty_grad, key_start, key_block, 1)
            reach_block = lax.dynamic_slice_in_dim(reach_sums, key_start, key_block, 0)
            grad_picked = reach_block[None, :] - jnp.cumsum(flow_block, axis=0)
            grad_select = grad_picked * strength * jax.nn.sigmoid(first_scores) * chosen
            grad_head = (
                lax.dynamic_slice_in_dim(first_grad, key_start, key_block, 1) + grad_select
            ).astype(jnp.bfloat16)
            grad_query_zero = grad_query_zero + matmul(grad_head, key_zero) * score_scale
            key_zero_grad = contract_rows(grad_head, query_zero) * score_scale
            grad_key_all = lax.dynamic_update_slice(
                grad_key_all, key_zero_grad, (key_start, jnp.zeros((), jnp.int32))
            )
            return (grad_query_zero, grad_key_all)

        grad_query_zero, grad_key_all = lax.fori_loop(
            0, block_total, head_block, (jnp.zeros((query_rows, HD), jnp.float32), grad_key_all)
        )
        grad_query = grad_query.at[:, 0, :].add(grad_query_zero).reshape(query_rows, model_width)
        grad_key_own, grad_value_own = (
            lax.psum_scatter(grad_key_all, "ctx", scatter_dimension=0, tiled=True),
            lax.psum_scatter(grad_value_all, "ctx", scatter_dimension=0, tiled=True),
        )
        grad_project = jnp.concatenate([grad_query, grad_key_own, grad_value_own], axis=1).astype(
            jnp.bfloat16
        )
        grad_qkv = contract_rows(normed_one, grad_project)
        grad_normed_one = contract_cols(grad_project, w_qkv_all)
        _, norm_one_back = jax.vjp(layer_norm, inputs, ln1_gain, ln1_bias)
        grad_in_part, grad_gain_one, grad_bias_one = norm_one_back(grad_normed_one)
        input_grads.append((grad_mid + grad_in_part).astype(jnp.bfloat16))
        matrix_grads = (grad_qkv, grad_outproj, grad_up, grad_down)
        vector_grads = (grad_gain_one, grad_bias_one, grad_gain_two, grad_bias_two, grad_bias_up)
        matrix_grads = (
            lax.psum_scatter(matrix_grads[0], "ctx", scatter_dimension=1, tiled=True),
            lax.psum_scatter(matrix_grads[1], "ctx", scatter_dimension=1, tiled=True),
            lax.psum_scatter(matrix_grads[2], "ctx", scatter_dimension=1, tiled=True),
            lax.psum_scatter(matrix_grads[3], "ctx", scatter_dimension=1, tiled=True),
        )
        matrix_grads = (
            lax.psum_scatter(
                matrix_grads[0].astype(jnp.bfloat16), "dp", scatter_dimension=0, tiled=True
            ).astype(jnp.float32),
            lax.psum_scatter(
                matrix_grads[1].astype(jnp.bfloat16), "dp", scatter_dimension=0, tiled=True
            ).astype(jnp.float32),
            lax.psum_scatter(
                matrix_grads[2].astype(jnp.bfloat16), "dp", scatter_dimension=0, tiled=True
            ).astype(jnp.float32),
            lax.psum_scatter(
                matrix_grads[3].astype(jnp.bfloat16), "dp", scatter_dimension=0, tiled=True
            ).astype(jnp.float32),
        )
        vector_grads = lax.psum(
            (vector_grads[0], vector_grads[1], vector_grads[2], vector_grads[3], vector_grads[4]),
            ("dp", "ctx"),
        )
        if matrix_total is None:
            matrix_total = matrix_grads
            vector_total = vector_grads
        else:
            matrix_total = tuple((old + new for old, new in zip(matrix_total, matrix_grads)))
            vector_total = tuple((old + new for old, new in zip(vector_total, vector_grads)))
    layer_out = jnp.stack(output_list)[:, None]
    input_out = jnp.stack(input_grads)[:, None]
    return (
        layer_out,
        input_out,
        vector_total[0],
        vector_total[1],
        matrix_total[0],
        matrix_total[1],
        vector_total[2],
        vector_total[3],
        matrix_total[2],
        vector_total[4],
        matrix_total[3],
    )


def solution(mesh):
    return jax.shard_map(
        on_device,
        mesh=mesh,
        in_specs=(
            P(None, "dp", "ctx", None),
            P(None, "dp", None),
            P(),
            P(),
            P("dp", None),
            P("dp", None),
            P(),
            P(),
            P("dp", None),
            P(),
            P("dp", None),
            P(None, "dp", "ctx", None),
        ),
        out_specs=(
            P(None, "dp", "ctx", None),
            P(None, "dp", "ctx", None),
            P(),
            P(),
            P("dp", "ctx"),
            P("dp", "ctx"),
            P(),
            P(),
            P("dp", "ctx"),
            P(),
            P("dp", "ctx"),
        ),
        check_vma=False,
    )
```

profile of v0, /device:TPU:0, one launch (start us, length us, event | category | flops | bytes accessed | tf_op | source)
XLA Modules:
  0.0 1941.8 jit_solution(4257634065860915347)
XLA Ops:
  10.5 32.6 %all-gather.13.cloned.1.call-done = bf16[768,2304]{1,0:T(8,128)(2,1)} async-done(((bf16[192,2304]{1,0:T(8,128)(2,1)}), bf16[768,2304]{1,0:T(8,128)(2,1)}) %all-gather.13.cloned.1.call-update) | async-done | bytes 3538960 | tf_op jit(solution)/shard_map/all_gather | solution.py:99
  58.3 32.6 %all-gather.27.cloned.1.call-done = bf16[1024,768]{1,0:T(8,128)(2,1)} async-done(((bf16[128,768]{1,0:T(8,128)(2,1)}), bf16[1024,768]{1,0:T(8,128)(2,1)}) %all-gather.27.cloned.1.call-update) | async-done | bytes 1572880 | tf_op jit(solution)/shard_map/all_gather | solution.py:113
  94.0 31.8 %all-gather.1 = f32[8192]{0:T(1024)S(1)} all-gather(f32[1024]{0:T(1024)S(1)} %get-tuple-element.1100), channel_id=3, replica_groups=mesh['dp'=4,'ctx'=8] {'ctx'}, dimensions={0}, use_global_device_ids=true | all-gather | bytes 36864 | tf_op jit(solution)/shard_map/all_gather | solution.py:18
  125.8 9.8 while.207
  138.8 14.8 while.200
  158.4 17.4 while.201
  175.8 6.8 all-gather.17.cloned.1.call-done
  182.7 3.1 while.196
  185.7 57.7 %all-gather = f32[8192]{0:T(1024)S(1)} all-gather(f32[1024]{0:T(1024)S(1)} %get-tuple-element.1095), channel_id=2, replica_groups=mesh['dp'=4,'ctx'=8] {'ctx'}, dimensions={0}, use_global_device_ids=true | all-gather | bytes 36864 | tf_op jit(solution)/shard_map/all_gather | solution.py:18
  243.5 9.8 while.206
  256.7 14.6 while.197
  275.9 16.7 while.198
  298.0 8.7 multiply_convert_fusion.6
  306.6 6.3 multiply_convert_fusion.7
  312.9 10.6 all-gather.23.cloned.1.call-done
  323.6 5.8 convert_reduce_fusion
  351.1 26.5 %while.204 = (s32[]{:T(128)}, f32[128,12,64]{0,2,1:T(8,128)}, f32[1024,768]{0,1:T(8,128)}, f32[1024,768]{0,1:T(8,128)}, f32[128,1024]{0,1:T(8,128)}, /*index=5*/...) while((s32[]{:T(128)}, f32[128,12,64]{0,2,1:T(8,128)}, ...), condition=%wide.region_59.60_spmd.clone, body=%wide.region_56.59_spmd.clone.sunk | while | flops 525927584 | bytes 110133752 | solution.py:261
  378.9 77.3 %all-gather.3 = f32[8192]{0:T(1024)S(1)} all-gather(f32[1024]{0:T(1024)S(1)} %reduce_sum.350), channel_id=5, replica_groups=mesh['dp'=4,'ctx'=8] {'ctx'}, dimensions={0}, use_global_device_ids=true | all-gather | bytes 36864 | tf_op jit(solution)/shard_map/all_gather | solution.py:18
  458.9 4.8 while.205
  470.9 25.0 %while.202 = (s32[]{:T(128)}, f32[128,12,64]{0,2,1:T(8,128)}, f32[1024,768]{0,1:T(8,128)}, f32[1024,768]{0,1:T(8,128)}, f32[128,1024]{0,1:T(8,128)}, /*index=5*/...) while((s32[]{:T(128)}, f32[128,12,64]{0,2,1:T(8,128)}, ...), condition=%wide.region_43.44_spmd.clone, body=%wide.region_40.43_spmd.clone.sunk | while | flops 525927584 | bytes 108536216 | solution.py:261
  497.1 60.6 %all-gather.2 = f32[8192]{0:T(1024)S(1)} all-gather(f32[1024]{0:T(1024)S(1)} %reduce_sum.341), channel_id=4, replica_groups=mesh['dp'=4,'ctx'=8] {'ctx'}, dimensions={0}, use_global_device_ids=true | all-gather | bytes 36864 | tf_op jit(solution)/shard_map/all_gather | solution.py:18
  558.9 4.1 while.203
  564.4 5.2 fusion.203
  570.9 5.2 fusion.202
  577.3 5.0 fusion.170
  583.4 5.0 fusion.176
  593.5 64.8 %reduce-scatter.33.cloned.1.call-done = f32[128,768]{0,1:T(8,128)} async-done(((f32[1024,768]{0,1:T(8,128)}), f32[128,768]{0,1:T(8,128)}) %reduce-scatter.33.cloned.1.call-update) | async-done | bytes 393232 | tf_op jit(solution)/shard_map/reduce_scatter | solution.py:301
  659.4 4.0 fusion.164
  664.4 71.6 %reduce-scatter.31.cloned.1.call-done = f32[128,768]{0,1:T(8,128)} async-done(((f32[1024,768]{0,1:T(8,128)}), f32[128,768]{0,1:T(8,128)}) %reduce-scatter.31.cloned.1.call-update) | async-done | bytes 393232 | tf_op jit(solution)/shard_map/reduce_scatter | solution.py:302
  737.0 76.8 %reduce-scatter.29.cloned.1.call-done = f32[128,768]{0,1:T(8,128)} async-done(((f32[1024,768]{0,1:T(8,128)}), f32[128,768]{0,1:T(8,128)}) %reduce-scatter.29.cloned.1.call-update) | async-done | bytes 393232 | tf_op jit(solution)/shard_map/reduce_scatter | solution.py:301
  815.5 4.6 fusion.166
  820.2 159.7 %reduce-scatter.49.cloned.1.call-done = f32[768,384]{1,0:T(8,128)} async-done(((f32[768,3072]{1,0:T(8,128)}), f32[768,384]{1,0:T(8,128)}) %reduce-scatter.49.cloned.1.call-update) | async-done | bytes 1179664 | tf_op jit(solution)/shard_map/reduce_scatter | solution.py:317
  982.1 163.8 %reduce-scatter.45.cloned.1.call-done = f32[768,384]{1,0:T(8,128)} async-done(((f32[768,3072]{1,0:T(8,128)}), f32[768,384]{1,0:T(8,128)}) %reduce-scatter.45.cloned.1.call-update) | async-done | bytes 1179664 | tf_op jit(solution)/shard_map/reduce_scatter | solution.py:317
  1148.2 163.8 %reduce-scatter.57.cloned.1.call-done = f32[3072,96]{0,1:T(8,128)} async-done(((f32[3072,768]{0,1:T(8,128)}), f32[3072,96]{0,1:T(8,128)}) %reduce-scatter.57.cloned.1.call-update) | async-done | bytes 1179664 | tf_op jit(solution)/shard_map/reduce_scatter | solution.py:318
  1314.2 3.1 fusion.134
  1317.3 160.7 %reduce-scatter.53.cloned.1.call-done = f32[3072,96]{0,1:T(8,128)} async-done(((f32[3072,768]{0,1:T(8,128)}), f32[3072,96]{0,1:T(8,128)}) %reduce-scatter.53.cloned.1.call-update) | async-done | bytes 1179664 | tf_op jit(solution)/shard_map/reduce_scatter | solution.py:318
  1480.3 3.2 fusion.135
  1484.4 14.9 reduce-scatter.67.cloned.1.call-done
  1500.2 21.2 %reduce-scatter.65.cloned.1.call-done = bf16[192,96]{1,0:T(8,128)(2,1)} async-done(((bf16[768,96]{1,0:T(8,128)(2,1)}), bf16[192,96]{1,0:T(8,128)(2,1)}) %reduce-scatter.65.cloned.1.call-update) | async-done | bytes 36880
  1523.1 3.4 fusion.165
  1528.0 126.1 %reduce-scatter.39.cloned.1.call-done = f32[768,288]{0,1:T(8,128)} async-done(((f32[768,2304]{0,1:T(8,128)}), f32[768,288]{0,1:T(8,128)}) %reduce-scatter.39.cloned.1.call-update) | async-done | bytes 884752 | tf_op jit(solution)/shard_map/reduce_scatter | solution.py:315
  1657.0 129.3 %reduce-scatter.37.cloned.1.call-done = f32[768,288]{0,1:T(8,128)} async-done(((f32[768,2304]{0,1:T(8,128)}), f32[768,288]{0,1:T(8,128)}) %reduce-scatter.37.cloned.1.call-update) | async-done | bytes 884752 | tf_op jit(solution)/shard_map/reduce_scatter | solution.py:315
  1788.7 40.2 %all-reduce = (f32[768]{0:T(1024)}, f32[768]{0:T(1024)}, f32[768]{0:T(1024)}, f32[768]{0:T(1024)}, f32[3072]{0:T(1024)}) all-reduce(f32[768]{0:T(1024)S(1)} %add.785, f32[768]{0:T(1024)S(1)} %add.786, f32[768]{0:T(1024)S(1)} %add.789, f32[768]{0:T(1024)S(1)} %add.790, f32[3072]{0:T(1024)S(1)} %add.792), channel_id=1, replica_groups=mesh['dp'=4,'ctx'=8] {'dp','ctx'}, use_global_device_ids=true, to_apply=%region_71.72 | all-reduce | flops 6144 | bytes 49152 | tf_op jit(solution)/shard_map/psum | solution.py:334
  1830.1 4.3 reduce-scatter.47.cloned.1.call-done
  1836.2 22.9 %reduce-scatter.59.cloned.1.call-done = bf16[768,96]{0,1:T(8,128)(2,1)} async-done(((bf16[3072,96]{0,1:T(8,128)(2,1)}), bf16[768,96]{0,1:T(8,128)(2,1)}) %reduce-scatter.59.cloned.1.call-update) | async-done | bytes 147472 | tf_op jit(solution)/shard_map/reduce_scatter | solution.py:330
  1859.0 24.5 %reduce-scatter.55.cloned.1.call-done = bf16[768,96]{0,1:T(8,128)(2,1)} async-done(((bf16[3072,96]{0,1:T(8,128)(2,1)}), bf16[768,96]{0,1:T(8,128)(2,1)}) %reduce-scatter.55.cloned.1.call-update) | async-done | bytes 147472 | tf_op jit(solution)/shard_map/reduce_scatter | solution.py:330
  1885.2 22.7 %reduce-scatter.63.cloned.1.call-done = bf16[192,288]{1,0:T(8,128)(2,1)} async-done(((bf16[768,288]{1,0:T(8,128)(2,1)}), bf16[192,288]{1,0:T(8,128)(2,1)}) %reduce-scatter.63.cloned.1.call-update) | async-done | bytes 110608
  1909.0 23.6 %reduce-scatter.61.cloned.1.call-done = bf16[192,288]{1,0:T(8,128)(2,1)} async-done(((bf16[768,288]{1,0:T(8,128)(2,1)}), bf16[192,288]{1,0:T(8,128)(2,1)}) %reduce-scatter.61.cloned.1.call-update) | async-done | bytes 110608
  (748 shorter events, 265.9 us)
Async XLA Ops:
  7.2 35.9 %all-gather.13.cloned.1.call-start = ((), (), s32[]{:S(2)}) async-start(), calls=%async_computation.20 | async-start | bytes 4423680 | tf_op jit(solution)/shard_map/all_gather | solution.py:99
  7.9 83.0 %all-gather.27.cloned.1.call-start = ((), (), s32[]{:S(2)}) async-start(), calls=%async_computation.27 | async-start | bytes 1769472 | tf_op jit(solution)/shard_map/all_gather | solution.py:113
  46.6 108.3 %all-gather.25.cloned.1.call-start = ((), (), s32[]{:S(2)}) async-start(), calls=%async_computation.26 | async-start | bytes 1769472 | tf_op jit(solution)/shard_map/all_gather | solution.py:114
  47.4 135.3 %all-gather.17.cloned.1.call-start = ((), (), s32[]{:S(2)}) async-start(), calls=%async_computation.22 | async-start | bytes 1769472 | tf_op jit(solution)/shard_map/all_gather | solution.py:113
  51.0 221.5 %all-gather.15.cloned.1.call-start = ((), (), s32[]{:S(2)}) async-start(), calls=%async_computation.21 | async-start | bytes 1769472 | tf_op jit(solution)/shard_map/all_gather | solution.py:114
  51.6 243.2 %all-gather.19.cloned.1.call-start = ((), (), s32[]{:S(2)}) async-start(), calls=%async_computation.23 | async-start | bytes 1474560 | tf_op jit(solution)/shard_map/all_gather | solution.py:100
  52.2 245.7 %all-gather.21.cloned.1.call-start = ((), (), s32[]{:S(2)}) async-start(), calls=%async_computation.24 | async-start | bytes 5898240 | tf_op jit(solution)/shard_map/all_gather | solution.py:101
  52.9 270.6 %all-gather.23.cloned.1.call-start = ((), (), s32[]{:S(2)}) async-start(), calls=%async_computation.25 | async-start | bytes 5898240 | tf_op jit(solution)/shard_map/all_gather | solution.py:102
  53.7 534.9 %reduce-scatter.43.cloned.1.call-start = ((), (), s32[]{:S(2)}) async-start(), calls=%async_computation.35 | async-start | bytes 2654208 | tf_op jit(solution)/shard_map/reduce_scatter | solution.py:316
  94.0 44.2 %copy-start.59 = (bf16[128,64]{1,0:T(8,128)(2,1)}, bf16[128,64]{1,0:T(8,128)(2,1)S(1)}, u32[]{:S(2)}) copy-start(bf16[128,64]{1,0:T(8,128)(2,1)S(1)} %get-tuple-element.3856) | copy-start | bytes 49156
  340.9 249.7 %reduce-scatter.41.cloned.1.call-start = ((), (), s32[]{:S(2)}) async-start(), calls=%async_computation.34 | async-start | bytes 2654208 | tf_op jit(solution)/shard_map/reduce_scatter | solution.py:316
  344.5 248.0 %reduce-scatter.35.cloned.1.call-start = ((), (), s32[]{:S(2)}) async-start(), calls=%async_computation.31 | async-start | bytes 3538944 | tf_op jit(solution)/shard_map/reduce_scatter | solution.py:302
  456.3 202.0 %reduce-scatter.33.cloned.1.call-start = ((), (), s32[]{:S(2)}) async-start(), calls=%async_computation.30 | async-start | bytes 3538944 | tf_op jit(solution)/shard_map/reduce_scatter | solution.py:301
  464.3 271.6 %reduce-scatter.31.cloned.1.call-start = ((), (), s32[]{:S(2)}) async-start(), calls=%async_computation.29 | async-start | bytes 3538944 | tf_op jit(solution)/shard_map/reduce_scatter | solution.py:302
  557.8 256.0 %reduce-scatter.29.cloned.1.call-start = ((), (), s32[]{:S(2)}) async-start(), calls=%async_computation.28 | async-start | bytes 3538944 | tf_op jit(solution)/shard_map/reduce_scatter | solution.py:301
  563.1 416.8 %reduce-scatter.49.cloned.1.call-start = ((), (), s32[]{:S(2)}) async-start(), calls=%async_computation.38 | async-start | bytes 10616832 | tf_op jit(solution)/shard_map/reduce_scatter | solution.py:317
  569.6 576.3 %reduce-scatter.45.cloned.1.call-start = ((), (), s32[]{:S(2)}) async-start(), calls=%async_computation.36 | async-start | bytes 10616832 | tf_op jit(solution)/shard_map/reduce_scatter | solution.py:317
  576.1 735.9 %reduce-scatter.57.cloned.1.call-start = ((), (), s32[]{:S(2)}) async-start(), calls=%async_computation.42 | async-start | bytes 10616832 | tf_op jit(solution)/shard_map/reduce_scatter | solution.py:318
  582.3 895.7 %reduce-scatter.53.cloned.1.call-start = ((), (), s32[]{:S(2)}) async-start(), calls=%async_computation.40 | async-start | bytes 10616832 | tf_op jit(solution)/shard_map/reduce_scatter | solution.py:318
  588.5 910.8 %reduce-scatter.67.cloned.1.call-start = ((), (), s32[]{:S(2)}) async-start(), calls=%async_computation.47 | async-start | bytes 245760
  590.4 68.9 %copy-start.14 = (bf16[2,1,128,768]{3,2,1,0:T(8,128)(2,1)S(1)}, bf16[2,1,128,768]{3,2,1,0:T(8,128)(2,1)}, u32[]{:S(2)}) copy-start(bf16[2,1,128,768]{3,2,1,0:T(8,128)(2,1)} %param.44) | copy-start | bytes 1179652
  590.4 68.9 %copy-start.106 = (f32[768]{0:T(1024)S(1)}, f32[768]{0:T(1024)}, u32[]{:S(2)}) copy-start(f32[768]{0:T(1024)} %param.46) | copy-start | bytes 9220
  590.4 69.0 %copy-start.116 = (f32[768]{0:T(1024)S(1)}, f32[768]{0:T(1024)}, u32[]{:S(2)}) copy-start(f32[768]{0:T(1024)} %param.47) | copy-start | bytes 9220
  590.4 69.0 %copy-start.124 = (f32[128]{0:T(128)S(1)}, f32[128]{0:T(128)}, u32[]{:S(2)}) copy-start(f32[128]{0:T(128)} %copy-done.123) | copy-start | bytes 1540
  590.4 69.0 %copy-start.139 = (f32[128]{0:T(128)S(1)}, f32[128]{0:T(128)}, u32[]{:S(2)}) copy-start(f32[128]{0:T(128)} %copy-done.138) | copy-start | bytes 1540
  590.4 931.0 %reduce-scatter.65.cloned.1.call-start = ((), (), s32[]{:S(2)}) async-start(), calls=%async_computation.46 | async-start | bytes 245760
  592.4 1061.7 %reduce-scatter.39.cloned.1.call-start = ((), (), s32[]{:S(2)}) async-start(), calls=%async_computation.33 | async-start | bytes 7962624 | tf_op jit(solution)/shard_map/reduce_scatter | solution.py:315
  593.5 69.9 %copy-start.80 = (bf16[128,768]{0,1:T(8,128)(2,1)}, bf16[128,768]{0,1:T(8,128)(2,1)S(1)}, u32[]{:S(2)}) copy-start(bf16[128,768]{0,1:T(8,128)(2,1)S(1)} %convert.25) | copy-start | bytes 589828
  663.4 152.1 %copy-start.126 = (f32[128]{0:T(128)S(1)}, f32[128]{0:T(128)}, u32[]{:S(2)}) copy-start(f32[128]{0:T(128)} %copy-done.125) | copy-start | bytes 1540
  663.4 1122.9 %reduce-scatter.37.cloned.1.call-start = ((), (), s32[]{:S(2)}) async-start(), calls=%async_computation.32 | async-start | bytes 7962624 | tf_op jit(solution)/shard_map/reduce_scatter | solution.py:315
  664.4 155.7 %copy-start.84 = (bf16[128,12,64]{0,2,1:T(8,128)(2,1)}, bf16[128,12,64]{0,2,1:T(8,128)(2,1)S(1)}, u32[]{:S(2)}) copy-start(bf16[128,12,64]{0,2,1:T(8,128)(2,1)S(1)} %convert.20) | copy-start | bytes 589828
  820.2 1009.9 %reduce-scatter.51.cloned.1.call-start = ((), (), s32[]{:S(2)}) async-start(), calls=%async_computation.39 | async-start | bytes 737280 | tf_op jit(solution)/shard_map/reduce_scatter | solution.py:327
  982.0 852.4 %reduce-scatter.47.cloned.1.call-start = ((), (), s32[]{:S(2)}) async-start(), calls=%async_computation.37 | async-start | bytes 737280 | tf_op jit(solution)/shard_map/reduce_scatter | solution.py:327
  1148.1 710.9 %reduce-scatter.59.cloned.1.call-start = ((), (), s32[]{:S(2)}) async-start(), calls=%async_computation.43 | async-start | bytes 737280 | tf_op jit(solution)/shard_map/reduce_scatter | solution.py:330
  1314.1 569.4 %reduce-scatter.55.cloned.1.call-start = ((), (), s32[]{:S(2)}) async-start(), calls=%async_computation.41 | async-start | bytes 737280 | tf_op jit(solution)/shard_map/reduce_scatter | solution.py:330
  1480.3 42.8 %copy-start.81 = (bf16[128,768]{0,1:T(8,128)(2,1)S(1)}, bf16[128,768]{0,1:T(8,128)(2,1)}, u32[]{:S(2)}) copy-start(bf16[128,768]{0,1:T(8,128)(2,1)} %copy-done.80) | copy-start | bytes 589828
  1480.3 42.8 %copy-start.83 = (bf16[128,768]{0,1:T(8,128)(2,1)S(1)}, bf16[128,768]{0,1:T(8,128)(2,1)}, u32[]{:S(2)}) copy-start(bf16[128,768]{0,1:T(8,128)(2,1)} %copy-done.82) | copy-start | bytes 589828
  1480.3 427.7 %reduce-scatter.63.cloned.1.call-start = ((), (), s32[]{:S(2)}) async-start(), calls=%async_computation.45 | async-start | bytes 737280
  1528.0 128.5 %copy-start.164 = (f32[128]{0:T(128)S(1)}, f32[128]{0:T(128)}, u32[]{:S(2)}) copy-start(f32[128]{0:T(128)} %copy-done.163) | copy-start | bytes 1540
  1528.0 128.5 %copy-start.162 = (f32[128]{0:T(128)S(1)}, f32[128]{0:T(128)}, u32[]{:S(2)}) copy-start(f32[128]{0:T(128)} %copy-done.161) | copy-start | bytes 1540
  1528.0 128.5 %copy-start.140 = (f32[128]{0:T(128)S(1)}, f32[128]{0:T(128)}, u32[]{:S(2)}) copy-start(f32[128]{0:T(128)} %copy-done.138) | copy-start | bytes 1540
  1528.0 128.5 %copy-start.142 = (f32[128]{0:T(128)S(1)}, f32[128]{0:T(128)}, u32[]{:S(2)}) copy-start(f32[128]{0:T(128)} %copy-done.141) | copy-start | bytes 1540
  1656.4 276.2 %reduce-scatter.61.cloned.1.call-start = ((), (), s32[]{:S(2)}) async-start(), calls=%async_computation.44 | async-start | bytes 737280
  1656.9 172.0 %copy-start.42 = (f32[128,768]{1,0:T(8,128)S(1)}, f32[128,768]{1,0:T(8,128)}, u32[]{:S(2)}) copy-start(f32[128,768]{1,0:T(8,128)} %copy-done.41) | copy-start | bytes 1179652
  1657.0 171.9 %copy-start.44 = (f32[128,768]{1,0:T(8,128)S(1)}, f32[128,768]{1,0:T(8,128)}, u32[]{:S(2)}) copy-start(f32[128,768]{1,0:T(8,128)} %copy-done.43) | copy-start | bytes 1179652
  1657.0 171.9 %copy-start.49 = (bf16[2,1,128,768]{3,2,1,0:T(8,128)(2,1)S(1)}, bf16[2,1,128,768]{3,2,1,0:T(8,128)(2,1)}, u32[]{:S(2)}) copy-start(bf16[2,1,128,768]{3,2,1,0:T(8,128)(2,1)} %param.55) | copy-start | bytes 1179652
  1657.0 171.9 %copy-start.148 = (f32[128]{0:T(128)S(1)}, f32[128]{0:T(128)}, u32[]{:S(2)}) copy-start(f32[128]{0:T(128)} %copy-done.147) | copy-start | bytes 1540
  1657.0 171.9 %copy-start.150 = (f32[128]{0:T(128)S(1)}, f32[128]{0:T(128)}, u32[]{:S(2)}) copy-start(f32[128]{0:T(128)} %copy-done.149) | copy-start | bytes 1540
  (151 other events, 772.9 us)
Sparse Core Ops, SparseCore 0:
  9.6 33.4 all-gather.12
  46.8 44.1 all-gather.26
  93.7 43.2 all-gather.24
  139.6 43.0 all-gather.16
  184.7 42.9 all-gather.14
  229.1 16.2 all-gather.18
  247.0 37.4 all-gather.20
  286.0 37.4 all-gather.22
  341.0 90.2 reduce-scatter.42
  434.6 68.1 reduce-scatter.40
  506.4 74.3 reduce-scatter.34
  584.3 73.9 reduce-scatter.32
  661.9 74.0 reduce-scatter.30
  739.5 74.3 reduce-scatter.28
  817.2 162.5 reduce-scatter.48
  983.3 162.5 reduce-scatter.44
  1149.4 162.5 reduce-scatter.56
  1315.4 162.5 reduce-scatter.52
  1480.4 18.8 reduce-scatter.66
  1501.6 19.7 reduce-scatter.64
  1525.1 128.9 reduce-scatter.38
  1658.2 128.0 reduce-scatter.36
  1788.8 21.1 reduce-scatter.50
  1812.4 22.0 reduce-scatter.46
  1836.9 22.0 reduce-scatter.58
  1861.4 22.0 reduce-scatter.54
  1885.8 22.0 reduce-scatter.62
  1910.4 22.0 reduce-scatter.60
where the time goes:
time: 1960 us; the launch traced here: 1940 us
  waiting for transfers between devices  1340 us (68%)
  blocking collectives  268 us (14%)
  local copies, waits for them, and re-layouts  113 us (6%)
  matrix products  110 us (6%)
  other arithmetic  92.4 us (5%)
    reduce_scatter x2, waiting for transfers between devices, on_device(): lax.psum_scatter(matrix_grads[3], 'ctx', scatter_dimension=1, tiled=True)  324 us
    reduce_scatter x2, waiting for transfers between devices, on_device(): lax.psum_scatter(matrix_grads[2], 'ctx', scatter_dimension=1, tiled=True)  323 us
    reduce_scatter x2, waiting for transfers between devices, on_device(): lax.psum_scatter(matrix_grads[0], 'ctx', scatter_dimension=1, tiled=True)  255 us
    all_gather x4, blocking collectives, prefix_2(): everything = lax.all_gather(array, axis)  227 us
    reduce_scatter x2, waiting for transfers between devices, on_device(): lax.psum_scatter(grad_key_all, 'ctx', scatter_dimension=0, tiled=True)  142 us
    unnamed x32, waiting for transfers between devices  86.5 us
    reduce_scatter x2, waiting for transfers between devices, on_device(): lax.psum_scatter(grad_value_all, 'ctx', scatter_dimension=0, tiled=True)  71.6 us
    reduce_scatter x2, waiting for transfers between devices, on_device(): lax.psum_scatter(matrix_grads[3].astype(jnp.bfloat16), 'dp', scatter_dime...  47.3 us
  transfers between devices with their start and end apart: 28, of which 20 were waited for; matrix products, arithmetic and copies ran while one was open for 14% of the time, Pallas kernels for 0%

commit v1 on v0

--- a/solution.py
+++ b/solution.py
@@ -1,8 +1,12 @@
+import math
 from functools import partial
+from types import SimpleNamespace
 
 import jax
 import jax.numpy as jnp
 from jax import lax
+from jax.experimental import pallas as pl
+from jax.experimental.pallas import tpu as pltpu
 from jax.sharding import PartitionSpec as P
 
 HD = 64
@@ -62,7 +66,7 @@
     return earlier + later
 
 
-def on_device(
+def per_token_device(
     layer_input,
     doc_lengths,
     ln1_gain,
@@ -358,6 +362,898 @@
     )
 
 
+MESH = pl.DeviceIdType.MESH
+EXCLUDED = 1e30
+QUERY_BLOCK = 256
+
+
+def whole(ref, peer):
+    return ref
+
+
+def piece(ref, peer):
+    return ref.at[peer]
+
+
+def exchange_body(jobs, sizes, *refs):
+    count = len(jobs)
+    sources, targets = refs[:count], refs[count : 2 * count]
+    send_sems, recv_sems = refs[2 * count : 3 * count], refs[3 * count : 4 * count]
+    local_sem = refs[4 * count]
+    barrier = pltpu.get_barrier_semaphore()
+    greeted = 0
+    for axis, size in sizes.items():
+        me = lax.axis_index(axis)
+        for step in range(1, size):
+            pl.semaphore_signal(
+                barrier, inc=1, device_id={axis: lax.rem(me + step, size)}, device_id_type=MESH
+            )
+            greeted += 1
+    own = []
+    for at, (axis, select) in enumerate(jobs):
+        me = lax.axis_index(axis)
+        copy = pltpu.make_async_copy(
+            select(sources[at], me), targets[at].at[me], local_sem.at[at]
+        )
+        copy.start()
+        own.append(copy)
+    pl.semaphore_wait(barrier, greeted)
+    sent = []
+    for at, (axis, select) in enumerate(jobs):
+        me, size = lax.axis_index(axis), sizes[axis]
+        for step in range(1, size):
+            peer = lax.rem(me + step, size)
+            copy = pltpu.make_async_remote_copy(
+                src_ref=select(sources[at], peer),
+                dst_ref=targets[at].at[me],
+                send_sem=send_sems[at].at[step - 1],
+                recv_sem=recv_sems[at].at[step - 1],
+                device_id={axis: peer},
+                device_id_type=MESH,
+            )
+            copy.start()
+            sent.append(copy)
+    for copy in own + sent:
+        copy.wait()
+
+
+def exchange(collective_id, name, *jobs):
+    arrays = [job[0] for job in jobs]
+    axes = [job[1] for job in jobs]
+    sizes = {axis: lax.axis_size(axis) for axis in axes}
+    count = len(jobs)
+    return pl.pallas_call(
+        partial(exchange_body, [(job[1], job[2]) for job in jobs], sizes),
+        out_shape=[
+            jax.ShapeDtypeStruct((sizes[axis],) + tuple(job[3]), job[0].dtype)
+            for axis, job in zip(axes, jobs)
+        ],
+        in_specs=[pl.BlockSpec(memory_space=pl.ANY)] * count,
+        out_specs=[pl.BlockSpec(memory_space=pl.ANY)] * count,
+        scratch_shapes=[pltpu.SemaphoreType.DMA((sizes[axis] - 1,)) for axis in axes] * 2
+        + [pltpu.SemaphoreType.DMA((count,))],
+        compiler_params=pltpu.CompilerParams(
+            collective_id=collective_id, has_side_effects=True
+        ),
+        name=name,
+    )(*arrays)
+
+
+def segment_of(places, ends_ref, doc_count):
+    total = jnp.zeros(places.shape, jnp.int32)
+    for at in range(doc_count):
+        total += jnp.where(places >= ends_ref[at], 1, 0)
+    return total
+
+
+def attend_body(hpg, strength, doc_count, ends_ref, proj_ref, probs_ref, slope_ref, out_ref, inv_ref, prefix):
+    rows_all = proj_ref.shape[0]
+    width = hpg * HD
+    block = QUERY_BLOCK
+    prefix[...] = jnp.zeros_like(prefix)
+    row_at = lax.broadcasted_iota(jnp.int32, (block, block), 0)
+    col_at = lax.broadcasted_iota(jnp.int32, (block, block), 1)
+    earlier = (col_at < row_at).astype(jnp.bfloat16)
+    scale = HD ** (-0.5)
+    for start in range(0, rows_all, block):
+        reach = start + block
+        rows = pl.ds(start, block)
+        row_pos = start + lax.broadcasted_iota(jnp.int32, (block, 1), 0)
+        col_pos = lax.broadcasted_iota(jnp.int32, (1, reach), 1)
+        row_seg = segment_of(row_pos, ends_ref, doc_count)
+        col_seg = segment_of(col_pos, ends_ref, doc_count)
+        before_seg = segment_of(col_pos - 1, ends_ref, doc_count)
+        opening = (col_seg != before_seg) | (col_pos == 0)
+        pick_seg = jnp.where(opening, -1, col_seg)
+        query = proj_ref[rows, 3 * width : 3 * width + HD] * scale
+        key = proj_ref[:reach, 3 * width + HD : 3 * width + 2 * HD]
+        scores = contract_cols(query.astype(jnp.bfloat16), key)
+        small = jnp.exp(-jnp.abs(scores))
+        soft = jnp.maximum(scores, 0.0) + jnp.log(1.0 + small)
+        recip = 1.0 / (1.0 + small)
+        sigmoid = jnp.where(scores >= 0.0, recip, small * recip)
+        chosen = (row_seg == pick_seg) & (col_pos < row_pos)
+        picked = jnp.where(chosen, strength * soft, 0.0)
+        slope_ref[rows, :reach] = jnp.where(chosen, strength * sigmoid, 0.0).astype(jnp.bfloat16)
+        high = picked.astype(jnp.bfloat16)
+        low = (picked - high.astype(jnp.float32)).astype(jnp.bfloat16)
+        penalty = prefix[:, :reach] + (matmul(earlier, high) + matmul(earlier, low))
+        allowed = (row_seg == col_seg) & (col_pos <= row_pos)
+        penalty = jnp.where(allowed, penalty, EXCLUDED)
+        prefix[:, :reach] += jnp.sum(picked, axis=0, keepdims=True)
+        for head in range(hpg):
+            at = head * HD
+            query = (proj_ref[rows, at : at + HD] * scale).astype(jnp.bfloat16)
+            key = proj_ref[:reach, width + at : width + at + HD]
+            value = proj_ref[:reach, 2 * width + at : 2 * width + at + HD]
+            logits = contract_cols(query, key) - penalty
+            top = jnp.max(logits, axis=1, keepdims=True)
+            probs = jnp.exp(logits - top)
+            inverse = 1.0 / jnp.sum(probs, axis=1, keepdims=True)
+            probs = probs.astype(jnp.bfloat16)
+            probs_ref[head, rows, :reach] = probs
+            out_ref[rows, at : at + HD] = matmul(probs, value) * inverse
+            inv_ref[rows, head : head + 1] = inverse
+
+
+def attend(ends, proj, hpg, strength):
+    rows = proj.shape[0]
+    vmem = pl.BlockSpec(memory_space=pltpu.VMEM)
+    return pl.pallas_call(
+        partial(attend_body, hpg, strength, ends.shape[0]),
+        out_shape=[
+            jax.ShapeDtypeStruct((hpg, rows, rows), jnp.bfloat16),
+            jax.ShapeDtypeStruct((rows, rows), jnp.bfloat16),
+            jax.ShapeDtypeStruct((rows, hpg * HD), jnp.float32),
+            jax.ShapeDtypeStruct((rows, hpg), jnp.float32),
+        ],
+        in_specs=[pl.BlockSpec(memory_space=pltpu.SMEM), vmem],
+        out_specs=[vmem] * 4,
+        scratch_shapes=[pltpu.VMEM((1, rows), jnp.float32)],
+        compiler_params=pltpu.CompilerParams(vmem_limit_bytes=48 * 1024 * 1024),
+        name="attend",
+    )(ends, proj)
+
+
+def norm_parts(value):
+    row_mean = jnp.mean(value, axis=-1, keepdims=True)
+    centered = value - row_mean
+    spread = jnp.mean(centered * centered, axis=-1, keepdims=True)
+    inverse = lax.rsqrt(spread + NORM_EPSILON)
+    return centered * inverse, inverse
+
+
+def norm_back(xhat, inverse, grad, gain):
+    scaled = grad * gain
+    return (
+        scaled
+        - jnp.mean(scaled, axis=-1, keepdims=True)
+        - xhat * jnp.mean(scaled * xhat, axis=-1, keepdims=True)
+    ) * inverse
+
+
+class Wires:
+    def __init__(self, send_sem, recv_sem):
+        self.send_sem, self.recv_sem, self.used, self.made = send_sem, recv_sem, 0, []
+
+    def send(self, source, target, where):
+        copy = pltpu.make_async_remote_copy(
+            src_ref=source,
+            dst_ref=target,
+            send_sem=self.send_sem.at[self.used],
+            recv_sem=self.recv_sem.at[self.used],
+            device_id=where,
+            device_id_type=MESH,
+        )
+        copy.start()
+        self.used += 1
+        self.made.append(copy)
+        return copy
+
+    def drain(self):
+        for copy in self.made:
+            copy.wait_send()
+
+
+def rounded(value):
+    return value.astype(jnp.bfloat16)
+
+
+def swap(index):
+    return index + 1 - 2 * lax.rem(index, 2)
+
+
+def rest_body(plan, names, *refs):
+    r = SimpleNamespace(**dict(zip(names, refs)))
+    groups, shards = plan
+    f32 = jnp.float32
+    ctx, dp = lax.axis_index("ctx"), lax.axis_index("dp")
+    ctx_size, tokens, width = r.att.shape
+    lines = ctx_size // 2
+    mbs = ctx_size // groups
+    hpg = width // HD
+    own, model = r.x.shape
+    ff = r.w_down_hbm.shape[0]
+    row_length = tokens * ctx_size
+    side, line = lax.rem(ctx, 2), ctx // 2
+    my_mb, my_group = ctx // groups, lax.rem(ctx, groups)
+    wires = Wires(r.send_sem, r.recv_sem)
+    core, far, far_core = {"dp": swap(dp)}, {"dp": lax.rem(dp + 2, 4)}, {"dp": lax.rem(swap(dp) + 2, 4)}
+    beside = {"ctx": swap(ctx)}
+    up_to = {"dp": lax.rem(ctx, 4), "ctx": shards * dp + ctx // 4}
+    up_from = {"dp": ctx // shards, "ctx": lax.rem(ctx, shards) * 4 + dp}
+    around = [{"ctx": lax.rem(ctx + step, ctx_size)} for step in range(1, ctx_size)]
+
+    loads = {}
+    for at, name in enumerate(("cot", "w_out", "w_up", "w_down", "probs", "slope", "proj", "out", "w_pick", "normed_one", "hat_one")):
+        loads[name] = pltpu.make_async_copy(
+            getattr(r, name + "_hbm"), getattr(r, name), r.load_sem.at[at]
+        )
+        loads[name].start()
+    barrier = pltpu.get_barrier_semaphore()
+    for where in around + [core, far, far_core, up_from]:
+        pl.semaphore_signal(barrier, inc=1, device_id=where, device_id_type=MESH)
+    pl.semaphore_wait(barrier, ctx_size + 3)
+
+    att_in = []
+    for step in range(1, ctx_size):
+        peer = lax.rem(ctx + step, ctx_size)
+        att_in.append(wires.send(r.att.at[peer], r.att_got.at[ctx], {"ctx": peer}))
+    loads["cot"].wait()
+    cot_core = wires.send(r.cot, r.cots.at[1], core)
+    cot_far = wires.send(r.cot, r.cots.at[2], far)
+    r.att_got[ctx] = r.att[ctx]
+    r.cots[0] = r.cot[...]
+    for name in ("w_out", "w_up", "w_down"):
+        loads[name].wait()
+    cot_far.wait_recv()
+    cot_fwd = wires.send(r.cots.at[2], r.cots.at[3], core)
+    for copy in att_in:
+        copy.wait_recv()
+
+    gain, bias = r.gain_two[...], r.bias_two[...]
+    for micro in range(mbs):
+        rows = pl.ds(micro * tokens, tokens)
+        stream = r.x[rows, :].astype(f32)
+        for group in range(groups):
+            stream += matmul(
+                r.att_got[micro * groups + group], r.w_out[pl.ds(group * width, width), :]
+            )
+        r.mid[rows, :] = stream
+    xhat, inverse_two = norm_parts(r.mid[...])
+    r.hat_two[...] = xhat
+    r.normed[0] = rounded(xhat * gain + bias)
+    to_core = wires.send(r.normed.at[0], r.normed.at[1], core)
+    to_far = wires.send(r.normed.at[0], r.normed.at[2], far)
+
+    def feed(slot):
+        hidden = matmul(r.normed[slot], r.w_up[...]) + r.b_up[...]
+        cdf = 0.5 * (1.0 + lax.erf(hidden * (2.0**-0.5)))
+        density = jnp.exp(-0.5 * hidden * hidden) * ((2.0 * math.pi) ** -0.5)
+        r.act[slot] = rounded(hidden * cdf)
+        grad = contract_cols(r.cots[slot], r.w_down[...])
+        r.grad_hid[slot] = rounded(grad * (cdf + hidden * density))
+        r.part[slot] = rounded(contract_cols(r.grad_hid[slot], r.w_up[...]))
+
+    def feed_out(slot):
+        r.out_part[slot] = rounded(matmul(r.act[slot], r.w_down[...]))
+
+    feed(0)
+    cot_core.wait_recv()
+    to_core.wait_recv()
+    feed(1)
+    part_core = wires.send(r.part.at[1], r.part_got.at[0], core)
+    to_far.wait_recv()
+    forward = wires.send(r.normed.at[2], r.normed.at[3], core)
+    feed(2)
+    forward.wait_recv()
+    cot_fwd.wait_recv()
+    feed(3)
+    part_far_core = wires.send(r.part.at[3], r.part_got.at[1], core)
+    feed_out(3)
+    out_far_core = wires.send(r.out_part.at[3], r.out_got.at[1], core)
+    part_far_core.wait_recv()
+    r.part[2] = rounded(r.part[2].astype(f32) + r.part_got[1].astype(f32))
+    part_far = wires.send(r.part.at[2], r.part_got.at[2], far)
+    feed_out(1)
+    out_core = wires.send(r.out_part.at[1], r.out_got.at[0], core)
+    feed_out(2)
+    out_far_core.wait_recv()
+    r.out_part[2] = rounded(r.out_part[2].astype(f32) + r.out_got[1].astype(f32))
+    out_far = wires.send(r.out_part.at[2], r.out_got.at[2], far)
+
+    flat_cot = r.cots[...].reshape(4 * own, model)
+    flat_act = r.act[...].reshape(4 * own, ff)
+    grads = rounded(contract_rows(flat_cot, flat_act))
+    size = model // ctx_size
+    for at in range(ctx_size):
+        r.down_grad[at % 2, at // 2] = grads[at * size : (at + 1) * size]
+    down_side = wires.send(r.down_grad.at[1 - side], r.down_side, beside)
+    flat_normed = r.normed[...].reshape(4 * own, model)
+    flat_grad = r.grad_hid[...].reshape(4 * own, ff)
+    size = model // 4
+    for at in range(shards):
+        grads = rounded(
+            contract_rows(flat_normed, flat_grad[:, at * ff // shards : (at + 1) * ff // shards])
+        )
+        for row in range(4):
+            index = at * 4 + row
+            r.up_grad[index % 2, index // 2] = grads[row * size : (row + 1) * size]
+    up_side = wires.send(r.up_grad.at[1 - side], r.up_side, beside)
+    feed_out(0)
+    vec_rows = 4 + ff // model
+    d_bias_up = jnp.sum(flat_grad.astype(f32), axis=0, keepdims=True)
+    for at in range(ff // model):
+        r.vec[4 + at : 5 + at, :] = d_bias_up[:, at * model : (at + 1) * model]
+
+    part_core.wait_recv()
+    part_far.wait_recv()
+    grad_normed = r.part[0].astype(f32) + r.part_got[0].astype(f32) + r.part_got[2].astype(f32)
+    xhat = r.hat_two[...]
+    r.vec[2:3, :] = jnp.sum(grad_normed * xhat, axis=0, keepdims=True)
+    r.vec[3:4, :] = jnp.sum(grad_normed, axis=0, keepdims=True)
+    r.grad_mid[...] = r.cot[...].astype(f32) + norm_back(xhat, inverse_two, grad_normed, gain)
+    branch = rounded(r.grad_mid[...])
+    for group in range(groups):
+        grad = rounded(contract_cols(branch, r.w_out[pl.ds(group * width, width), :]))
+        for micro in range(mbs):
+            r.att_out[micro * groups + group] = grad[micro * tokens : (micro + 1) * tokens]
+    att_in = []
+    for step in range(1, ctx_size):
+        peer = lax.rem(ctx + step, ctx_size)
+        att_in.append(wires.send(r.att_out.at[peer], r.grad_att.at[ctx], {"ctx": peer}))
+    r.grad_att[ctx] = r.att_out[ctx]
+    for group in range(groups):
+        total = None
+        for micro in range(mbs):
+            some = contract_rows(
+                branch[micro * tokens : (micro + 1) * tokens], r.att_got[micro * groups + group]
+            )
+            total = some if total is None else total + some
+        r.out_grad[group] = rounded(total)
+    out_grad_core = wires.send(r.out_grad.at[swap(dp)], r.out_grad_got.at[0], core)
+    out_grad_far_core = wires.send(
+        r.out_grad.at[lax.rem(swap(dp) + 2, 4)], r.out_grad_got.at[1], core
+    )
+    out_core.wait_recv()
+    out_far.wait_recv()
+    r.layer[...] = rounded(
+        r.mid[...]
+        + (r.out_part[0].astype(f32) + r.out_got[0].astype(f32) + r.out_got[2].astype(f32))
+    )
+    out_grad_far_core.wait_recv()
+    mine = lax.rem(dp + 2, 4)
+    r.out_grad[mine] = rounded(r.out_grad[mine].astype(f32) + r.out_grad_got[1].astype(f32))
+    out_grad_far = wires.send(r.out_grad.at[mine], r.out_grad_got.at[2], far)
+    for name in ("probs", "slope", "proj", "out", "w_pick", "normed_one", "hat_one"):
+        loads[name].wait()
+    for copy in att_in:
+        copy.wait_recv()
+
+    def spread(side_copy, grad, side_got, ready, line_got):
+        side_copy.wait_recv()
+        for step in range(lines):
+            place = lax.rem(line + step, lines)
+            ready[place] = rounded(grad[side, place].astype(f32) + side_got[place].astype(f32))
+        return [
+            wires.send(
+                ready.at[lax.rem(line + step, lines)],
+                line_got.at[line],
+                {"ctx": lax.rem(line + step, lines) * 2 + side},
+            )
+            for step in range(1, lines)
+        ]
+
+    def gather_up(copies, ready, line_got):
+        line_got[line] = ready[line]
+        for copy in copies:
+            copy.wait_recv()
+        total = line_got[0].astype(f32)
+        for place in range(1, lines):
+            total += line_got[place].astype(f32)
+        return total
+
+    block = QUERY_BLOCK
+    per_block = block // tokens
+    scale = HD ** (-0.5)
+    r.suffix[...] = jnp.zeros_like(r.suffix)
+    r.acc[...] = jnp.zeros_like(r.acc)
+    row_at = lax.broadcasted_iota(jnp.int32, (block, block), 0)
+    col_at = lax.broadcasted_iota(jnp.int32, (block, block), 1)
+    later = (col_at > row_at).astype(jnp.bfloat16)
+
+    def back_block(start):
+        reach = start + block
+        rows = pl.ds(start, block)
+        total = None
+        first = start // tokens
+        grad_block = r.grad_att[first : first + per_block].reshape(block, width)
+        for head in range(hpg):
+            at = head * HD
+            query_t = rounded((r.proj[rows, at : at + HD].astype(f32) * scale).T)
+            key = r.proj[:reach, width + at : width + at + HD]
+            value = r.proj[:reach, 2 * width + at : 2 * width + at + HD]
+            grad = grad_block[:, at : at + HD].astype(f32) * r.inverse[rows, head : head + 1]
+            delta = jnp.sum(grad * r.out[rows, at : at + HD], axis=1, keepdims=True)
+            probs = r.probs[head, rows, :reach]
+            grad_probs = contract_cols(rounded(grad), value)
+            grad_logits = probs.astype(f32) * (grad_probs - delta)
+            total = grad_logits if total is None else total + grad_logits
+            grad_scores = rounded(grad_logits)
+            r.grad_proj[rows, at : at + HD] = rounded(matmul(grad_scores, key) * scale)
+            r.acc[at : at + HD, :reach] += matmul(query_t, grad_scores)
+            r.acc[width + at : width + at + HD, :reach] += matmul(rounded(grad.T), probs)
+        query_t = rounded((r.proj[rows, 3 * width : 3 * width + HD].astype(f32) * scale).T)
+        key = r.proj[:reach, 3 * width + HD : 3 * width + 2 * HD]
+        flow = r.suffix[:, :reach] + matmul(later, rounded(total))
+        grad_scores = rounded(-flow * r.slope[rows, :reach].astype(f32))
+        r.grad_proj[rows, 3 * width : 3 * width + HD] = rounded(matmul(grad_scores, key) * scale)
+        r.acc[2 * width : 2 * width + HD, :reach] += matmul(query_t, grad_scores)
+        r.suffix[:, :reach] += jnp.sum(total, axis=0, keepdims=True)
+
+    starts = list(reversed(range(0, row_length, block)))
+    back_block(starts[0])
+    down_line = spread(down_side, r.down_grad, r.down_side, r.down_ready, r.down_line)
+    for start in starts[1:-1]:
+        back_block(start)
+    up_line = spread(up_side, r.up_grad, r.up_side, r.up_ready, r.up_line)
+    out_grad_core.wait_recv()
+    out_grad_far.wait_recv()
+    grads = rounded(
+        r.out_grad[dp].astype(f32) + r.out_grad_got[0].astype(f32) + r.out_grad_got[2].astype(f32)
+    )
+    size = model // ctx_size
+    for at in range(ctx_size):
+        r.out_piece[at % 2, at // 2] = grads[at * size : (at + 1) * size]
+    out_side = wires.send(r.out_piece.at[1 - side], r.out_side, beside)
+    back_block(starts[-1])
+    r.grad_kv[...] = rounded(r.acc[...])
+    r.grad_proj[:, width : 3 * width] = rounded(r.acc[: 2 * width, :].T)
+    r.grad_proj[:, 3 * width + HD :] = rounded(r.acc[2 * width :, :].T)
+
+    def one_piece(place, add):
+        rows = pl.ds(pl.multiple_of(place * tokens, tokens), tokens)
+        grad = contract_cols(r.grad_proj[rows, :], r.w_pick[...])
+        gain_sum = jnp.sum(grad * r.hat_one[rows, :].astype(f32), axis=0, keepdims=True)
+        bias_sum = jnp.sum(grad, axis=0, keepdims=True)
+        r.vec[0:1, :] = r.vec[0:1, :] + gain_sum if add else gain_sum
+        r.vec[1:2, :] = r.vec[1:2, :] + bias_sum if add else bias_sum
+        return grad
+
+    one_side = []
+    for step in range(lines):
+        place = lax.rem(line + lines - 1 - step, lines)
+        r.one_piece[step] = rounded(one_piece(place * 2 + 1 - side, step > 0))
+        one_side.append(wires.send(r.one_piece.at[step], r.one_side.at[step], beside))
+    for step in range(lines):
+        place = lax.rem(line + lines - 1 - step, lines)
+        r.one_own[step] = one_piece(place * 2 + side, True)
+    one_line = []
+    for step in range(lines):
+        place = lax.rem(line + lines - 1 - step, lines)
+        one_side[step].wait_recv()
+        r.one_ready[step] = rounded(r.one_own[step] + r.one_side[step].astype(f32))
+        if step < lines - 1:
+            one_line.append(
+                wires.send(r.one_ready.at[step], r.one_line.at[line], {"ctx": place * 2 + side})
+            )
+    r.one_line[line] = r.one_ready[lines - 1]
+    vec_in = []
+    for step in range(1, ctx_size):
+        peer = lax.rem(ctx + step, ctx_size)
+        vec_in.append(wires.send(r.vec, r.vec_got.at[ctx], {"ctx": peer}))
+    r.vec_got[ctx] = r.vec[...]
+
+    size = model // 4
+    grads_q = rounded(
+        contract_rows(
+            jnp.concatenate(
+                [r.grad_proj[:, :width], r.grad_proj[:, 3 * width : 3 * width + HD]], axis=1
+            ),
+            r.normed_one[...],
+        )
+    )
+    for at in range(4):
+        cols = slice(at * size, (at + 1) * size)
+        r.qkv_grad[at, :width, :] = grads_q[:width, cols]
+        r.qkv_grad[at, 3 * width : 3 * width + HD, :] = grads_q[width:, cols]
+    grads_kv = rounded(matmul(r.grad_kv[...], r.normed_one[...]))
+    for at in range(4):
+        cols = slice(at * size, (at + 1) * size)
+        r.qkv_grad[at, width : 3 * width, :] = grads_kv[: 2 * width, cols]
+        r.qkv_grad[at, 3 * width + HD :, :] = grads_kv[2 * width :, cols]
+    qkv_far_core = wires.send(r.qkv_grad.at[lax.rem(swap(dp) + 2, 4)], r.qkv_got.at[1], core)
+    qkv_core = wires.send(r.qkv_grad.at[swap(dp)], r.qkv_got.at[0], core)
+
+    r.d_down[...] = gather_up(down_line, r.down_ready, r.down_line).T
+    r.up_sum[...] = rounded(gather_up(up_line, r.up_ready, r.up_line))
+    stays = (lax.rem(ctx, 4) == dp) & (shards * dp + ctx // 4 == ctx)
+    up_copy = pltpu.make_async_remote_copy(
+        src_ref=r.up_sum,
+        dst_ref=r.up_final,
+        send_sem=r.up_send.at[0],
+        recv_sem=r.up_recv.at[0],
+        device_id=up_to,
+        device_id_type=MESH,
+    )
+
+    @pl.when(jnp.logical_not(stays))
+    def _():
+        up_copy.start()
+
+    @pl.when(stays)
+    def _():
+        r.up_final[...] = r.up_sum[...]
+
+    qkv_far_core.wait_recv()
+    r.qkv_grad[mine] = rounded(r.qkv_grad[mine].astype(f32) + r.qkv_got[1].astype(f32))
+    qkv_far = wires.send(r.qkv_grad.at[mine], r.qkv_got.at[2], far)
+    out_line = spread(out_side, r.out_piece, r.out_side, r.out_ready, r.out_line)
+    for copy in vec_in:
+        copy.wait_recv()
+    total = r.vec_got[0]
+    for at in range(1, ctx_size):
+        total += r.vec_got[at]
+    r.vec_sum[...] = total
+    vec_out = [
+        wires.send(r.vec_sum, r.vecs.at[dp], where) for where in (core, far, far_core)
+    ]
+    r.vecs[dp] = total
+    qkv_core.wait_recv()
+    qkv_far.wait_recv()
+    r.qkv_sum[...] = rounded(
+        r.qkv_grad[dp].astype(f32) + r.qkv_got[0].astype(f32) + r.qkv_got[2].astype(f32)
+    )
+    part = r.deal_got.shape[2]
+    per = width // part
+    slots = r.deal_got.shape[0]
+
+    def outgoing(kind, half):
+        section = (kind * groups + my_group) * per + half
+        target, slot = section // slots, lax.rem(section, slots)
+        index = kind * per + half
+        return target, slot, index, pltpu.make_async_remote_copy(
+            src_ref=r.qkv_sum.at[pl.ds(index * part, part)],
+            dst_ref=r.deal_got.at[slot, my_mb],
+            send_sem=r.deal_send.at[index],
+            recv_sem=r.deal_recv.at[slot, my_mb],
+            device_id={"ctx": target},
+            device_id_type=MESH,
+        )
+
+    def extra_copy(kind):
+        return pltpu.make_async_remote_copy(
+            src_ref=r.qkv_sum.at[pl.ds(3 * width + kind * HD, HD)],
+            dst_ref=r.extra_got.at[ctx],
+            send_sem=r.extra_send.at[kind],
+            recv_sem=r.extra_recv.at[ctx],
+            device_id={"ctx": kind * groups * per // slots},
+            device_id_type=MESH,
+        )
+
+    for kind in range(3):
+        for half in range(per):
+            target, slot, index, copy = outgoing(kind, half)
+
+            @pl.when(target != ctx)
+            def _():
+                copy.start()
+
+            @pl.when(target == ctx)
+            def _():
+                r.deal_got[slot, my_mb] = r.qkv_sum[index * part : (index + 1) * part, :]
+
+    for kind in range(2):
+        target = kind * groups * per // slots
+        copy = extra_copy(kind)
+
+        @pl.when(ctx != target)
+        def _():
+            copy.start()
+
+        @pl.when(ctx == target)
+        def _():
+            r.extra_got[ctx] = r.qkv_sum[3 * width + kind * HD : 3 * width + (kind + 1) * HD, :]
+
+    xhat, inverse_one = norm_parts(r.x[...].astype(f32))
+    gain_one = r.gain_one[...]
+    for copy in one_line:
+        copy.wait_recv()
+    half_lines = lines // mbs
+    for micro in range(mbs):
+        grad = r.one_line[micro * half_lines].astype(f32)
+        for at in range(1, half_lines):
+            grad += r.one_line[micro * half_lines + at].astype(f32)
+        rows = slice(micro * tokens, (micro + 1) * tokens)
+        r.d_x[rows, :] = rounded(
+            r.grad_mid[rows, :] + norm_back(xhat[rows], inverse_one[rows], grad, gain_one)
+        )
+    r.d_out[...] = gather_up(out_line, r.out_ready, r.out_line).T
+
+    @pl.when(jnp.logical_not(stays))
+    def _():
+        up_copy.wait_send()
+        up_copy.wait_recv()
+
+    r.d_up[...] = r.up_final[...].astype(f32)
+
+    for kind in range(3):
+        for half in range(per):
+            target, slot, index, copy = outgoing(kind, half)
+
+            @pl.when(target != ctx)
+            def _():
+                copy.wait_send()
+
+    for slot in range(slots):
+        section = ctx * slots + slot
+        source_group = lax.rem(section // per, groups)
+        for place in range(mbs):
+
+            @pl.when(place * groups + source_group != ctx)
+            def _():
+                pltpu.make_async_copy(
+                    r.qkv_sum.at[pl.ds(0, part)],
+                    r.deal_got.at[slot, place],
+                    r.deal_recv.at[slot, place],
+                ).wait()
+
+        total = r.deal_got[slot, 0].astype(f32)
+        for place in range(1, mbs):
+            total += r.deal_got[slot, place].astype(f32)
+        r.deal_sum[slot * part : (slot + 1) * part, :] = total
+    for kind in range(2):
+        section = kind * groups * per
+        target, slot = section // slots, section % slots
+        copy = extra_copy(kind)
+
+        @pl.when(ctx != target)
+        def _():
+            copy.wait_send()
+
+        @pl.when(ctx == target)
+        def _():
+            total = jnp.zeros((HD, size), f32)
+            for place in range(ctx_size):
+                if place != target:
+                    pltpu.make_async_copy(
+                        r.qkv_sum.at[pl.ds(0, HD)], r.extra_got.at[place], r.extra_recv.at[place]
+                    ).wait()
+                total += r.extra_got[place].astype(f32)
+            r.deal_sum[slot * part : slot * part + HD, :] += total
+
+    r.d_qkv[...] = r.deal_sum[...].T
+    for copy in vec_out:
+        copy.wait_recv()
+    for row in range(4):
+        r.d_vec[row : row + 1, :] = (
+            r.vecs[0, row : row + 1, :] + r.vecs[1, row : row + 1, :]
+        ) + (r.vecs[2, row : row + 1, :] + r.vecs[3, row : row + 1, :])
+    for at in range(4):
+        r.d_bias[at] = r.vecs[at, 4:vec_rows, :]
+    wires.drain()
+
+
+REST_COPIES = 72
+
+
+def rest(collective_id, groups, shards, small, large):
+    bf16, f32 = jnp.bfloat16, jnp.float32
+    att, x_own = small["att"], small["x"]
+    ctx_size, tokens, width = att.shape
+    own, model = x_own.shape
+    row_length = ctx_size * tokens
+    lines = ctx_size // 2
+    ff = large["w_down"].shape[0]
+    size, shard = model // 4, 3 * model // ctx_size
+    part = math.gcd(width, shard)
+    slots, mbs = shard // part, ctx_size // groups
+    picked = large["w_pick"].shape[1]
+    vec_rows = 4 + ff // model
+    narrow = model // ctx_size
+    vmem = pl.BlockSpec(memory_space=pltpu.VMEM)
+    anywhere = pl.BlockSpec(memory_space=pl.ANY)
+    outs = {
+        "layer": ((own, model), bf16),
+        "d_x": ((own, model), bf16),
+        "d_vec": ((4, model), f32),
+        "d_bias": ((4, ff // model, model), f32),
+        "d_qkv": ((size, shard), f32),
+        "d_out": ((size, narrow), f32),
+        "d_up": ((size, ff // shards), f32),
+        "d_down": ((ff, narrow), f32),
+    }
+    scratch = {name: (array.shape, array.dtype) for name, array in large.items()}
+    scratch |= {
+        "att_got": (att.shape, bf16),
+        "cots": ((4, own, model), bf16),
+        "mid": ((own, model), f32),
+        "hat_two": ((own, model), f32),
+        "grad_mid": ((own, model), f32),
+        "normed": ((4, own, model), bf16),
+        "act": ((4, own, ff), bf16),
+        "grad_hid": ((4, own, ff), bf16),
+        "part": ((4, own, model), bf16),
+        "out_part": ((4, own, model), bf16),
+        "part_got": ((3, own, model), bf16),
+        "out_got": ((3, own, model), bf16),
+        "att_out": (att.shape, bf16),
+        "grad_att": (att.shape, bf16),
+        "down_grad": ((2, lines, narrow, ff), bf16),
+        "down_side": ((lines, narrow, ff), bf16),
+        "down_ready": ((lines, narrow, ff), bf16),
+        "down_line": ((lines, narrow, ff), bf16),
+        "up_grad": ((2, lines, size, ff // shards), bf16),
+        "up_side": ((lines, size, ff // shards), bf16),
+        "up_ready": ((lines, size, ff // shards), bf16),
+        "up_line": ((lines, size, ff // shards), bf16),
+        "up_sum": ((size, ff // shards), bf16),
+        "up_final": ((size, ff // shards), bf16),
+        "out_grad": ((4, model, size), bf16),
+        "out_grad_got": ((3, model, size), bf16),
+        "out_piece": ((2, lines, narrow, size), bf16),
+        "out_side": ((lines, narrow, size), bf16),
+        "out_ready": ((lines, narrow, size), bf16),
+        "out_line": ((lines, narrow, size), bf16),
+        "suffix": ((1, row_length), f32),
+        "acc": ((2 * width + HD, row_length), f32),
+        "grad_kv": ((2 * width + HD, row_length), bf16),
+        "grad_proj": ((row_length, picked), bf16),
+        "one_piece": ((lines, tokens, model), bf16),
+        "one_own": ((lines, tokens, model), f32),
+        "one_side": ((lines, tokens, model), bf16),
+        "one_ready": ((lines, tokens, model), bf16),
+        "one_line": ((lines, tokens, model), bf16),
+        "qkv_grad": ((4, picked, size), bf16),
+        "qkv_got": ((3, picked, size), bf16),
+        "qkv_sum": ((picked, size), bf16),
+        "deal_got": ((slots, mbs, part, size), bf16),
+        "deal_sum": ((shard, size), f32),
+        "extra_got": ((ctx_size, HD, size), bf16),
+        "vec": ((vec_rows, model), f32),
+        "vec_got": ((ctx_size, vec_rows, model), f32),
+        "vec_sum": ((vec_rows, model), f32),
+        "vecs": ((4, vec_rows, model), f32),
+    }
+    dma = pltpu.SemaphoreType.DMA
+    sems = {
+        "send_sem": dma((REST_COPIES,)),
+        "recv_sem": dma((REST_COPIES,)),
+        "load_sem": dma((len(large),)),
+        "up_send": dma((1,)),
+        "up_recv": dma((1,)),
+        "deal_send": dma((3 * (width // part),)),
+        "deal_recv": dma((slots, mbs)),
+        "extra_send": dma((2,)),
+        "extra_recv": dma((ctx_size,)),
+    }
+    names = list(small) + [name + "_hbm" for name in large] + list(outs) + list(scratch) + list(sems)
+    return pl.pallas_call(
+        partial(rest_body, (groups, shards), names),
+        out_shape=[jax.ShapeDtypeStruct(*spec) for spec in outs.values()],
+        in_specs=[vmem] * len(small) + [anywhere] * len(large),
+        out_specs=[vmem] * len(outs),
+        scratch_shapes=[pltpu.VMEM(*spec) for spec in scratch.values()] + list(sems.values()),
+        compiler_params=pltpu.CompilerParams(
+            collective_id=collective_id, has_side_effects=True, vmem_limit_bytes=60 * 1024 * 1024
+        ),
+        name="rest",
+    )(*small.values(), *large.values())
+
+
+def per_head_device(
+    layer_input,
+    doc_lengths,
+    ln1_gain,
+    ln1_bias,
+    w_qkv,
+    w_out,
+    ln2_gain,
+    ln2_bias,
+    w_up,
+    b_up,
+    w_down,
+    cotangent,
+):
+    bf16, f32 = jnp.bfloat16, jnp.float32
+    mbs, _, tokens, model = layer_input.shape
+    ctx_size, dp_size = lax.axis_size("ctx"), lax.axis_size("dp")
+    ctx, dp = lax.axis_index("ctx"), lax.axis_index("dp")
+    row_length = tokens * ctx_size
+    groups = ctx_size // mbs
+    hpg = model // HD // groups
+    width = hpg * HD
+    strength = 8.0 / row_length
+    my_mb, grp = ctx // groups, lax.rem(ctx, groups)
+    ff_own = b_up.shape[0] // dp_size
+    x_own = layer_input[:, 0]
+    cot_own = cotangent[:, 0].reshape(mbs * tokens, model)
+    w_pick = jnp.concatenate(
+        [lax.dynamic_slice_in_dim(w_qkv, kind * model + grp * width, width, 1) for kind in range(3)]
+        + [w_qkv[:, :HD], w_qkv[:, model : model + HD]],
+        axis=1,
+    )
+
+    def peer_mb(ref, peer):
+        return ref.at[peer // groups]
+
+    def peer_columns(ref, peer):
+        return ref.at[:, pl.ds(pl.multiple_of(peer * ff_own, 128), ff_own)]
+
+    x_row, w_pick, w_up_own, w_out_all = exchange(
+        0,
+        "gather_start",
+        (x_own, "ctx", peer_mb, (tokens, model)),
+        (w_pick, "dp", whole, w_pick.shape),
+        (w_up, "dp", peer_columns, (w_up.shape[0], ff_own)),
+        (w_out, "dp", whole, w_out.shape),
+    )
+    x_row = x_row.reshape(row_length, model).astype(f32)
+    w_pick = w_pick.reshape(model, -1)
+    w_up_own = w_up_own.reshape(model, ff_own)
+    w_out_all = w_out_all.reshape(model, model)
+    xhat_row, _ = norm_parts(x_row)
+    normed_one = (xhat_row * ln1_gain + ln1_bias).astype(bf16)
+    proj = matmul(normed_one, w_pick).astype(bf16)
+    lengths = lax.dynamic_index_in_dim(doc_lengths[:, 0], my_mb, 0, keepdims=False)
+    ends = jnp.cumsum(lengths).astype(jnp.int32)
+    probs, slope, out, inverse = attend(ends, proj, hpg, strength)
+    shards = ctx_size // dp_size
+    small = {
+        "att": out.astype(bf16).reshape(ctx_size, tokens, width),
+        "x": x_own.reshape(mbs * tokens, model),
+        "inverse": inverse,
+        "b_up": lax.dynamic_slice_in_dim(b_up, dp * ff_own, ff_own, 0)[None],
+        "gain_one": ln1_gain[None],
+        "gain_two": ln2_gain[None],
+        "bias_two": ln2_bias[None],
+    }
+    large = {
+        "cot": cot_own,
+        "w_out": w_out_all,
+        "w_up": w_up_own,
+        "w_down": w_down,
+        "probs": probs,
+        "slope": slope,
+        "proj": proj,
+        "out": out,
+        "w_pick": w_pick,
+        "normed_one": normed_one,
+        "hat_one": xhat_row.astype(bf16),
+    }
+    layer_out, d_x, d_vec, d_bias, d_qkv, d_out, d_up, d_down = rest(1, groups, shards, small, large)
+    return (
+        layer_out.reshape(mbs, 1, tokens, model),
+        d_x.reshape(mbs, 1, tokens, model),
+        d_vec[0],
+        d_vec[1],
+        d_qkv,
+        d_out,
+        d_vec[2],
+        d_vec[3],
+        d_up,
+        d_bias.reshape(-1),
+        d_down,
+    )
+
+
+def on_device(*arguments):
+    layer_input = arguments[0]
+    mbs, model = layer_input.shape[0], layer_input.shape[3]
+    heads, ctx_size, dp_size = model // HD, lax.axis_size("ctx"), lax.axis_size("dp")
+    groups = ctx_size // mbs
+    fits = (
+        ctx_size % mbs == 0
+        and heads % groups == 0
+        and dp_size == 4
+        and ctx_size % dp_size == 0
+        and ctx_size == 8
+        and mbs == 2
+        and (layer_input.shape[2] * ctx_size) % QUERY_BLOCK == 0
+    )
+    return (per_head_device if fits else per_token_device)(*arguments)
+
+
 def solution(mesh):
     return jax.shard_map(
         on_device,

time: 1960 us -> 242 us (0.12)
  waiting for transfers between devices: 1340 us -> 0 us
  blocking collectives: 268 us -> 0 us
  Pallas kernels: 0 us -> 204 us
  matrix products: 110 us -> 1.4 us
  local copies, waits for them, and re-layouts: 113 us -> 22.6 us
  other arithmetic: 92.4 us -> 7.94 us
    reduce_scatter x16 -> x0, waiting for transfers between devices: 1170 us -> none  [the longest x2 324 us: on_device(): lax.psum_scatter(matrix_grads[3], 'ctx', scatter_dimension=1, tiled=True)]
    all_gather x4 -> x0, blocking collectives: 227 us -> none  [prefix_2(): everything = lax.all_gather(array, axis)]
    pallas_call x0 -> x3, Pallas kernels: none -> 204 us  [the longest x1 149 us: rest(): pl.pallas_call(partial(rest_body, (groups, shards), names), out_shape=[ja...]
    unnamed x32 -> x0, waiting for transfers between devices: 86.5 us -> none
    all_gather x8 -> x0, waiting for transfers between devices: 82.8 us -> none  [the longest x2 39.5 us: on_device(): lax.all_gather(projected[:, model_width:2 * model_width], 'ctx', axis=0,...]
    dot_general x38 -> x0, matrix products: 79 us -> none  [the longest x10 34.7 us: contract_rows(): lax.dot_general(left, right, (((0,), (0,)), ((), ())), preferred_element_...]
    psum x1 -> x0, blocking collectives: 40.2 us -> none  [on_device(): lax.psum((vector_grads[0], vector_grads[1], vector_grads[2], vector_grads...]
    dot_general x10 -> x1, matrix products: 31.3 us -> 1.4 us  [matmul(): return jnp.dot(left, right, preferred_element_type=jnp.float32)]
  transfers between devices with their start and end apart: 28 -> 0, of which waited for: 20 -> 0; matrix products, arithmetic and copies ran while one was open for 14% -> 0% of each run, Pallas kernels for 0% -> 0%
where the time goes in v1:
time: 242 us; the launch traced here: 237 us
  Pallas kernels  204 us (84%)
  local copies, waits for them, and re-layouts  22.6 us (9%)
  other arithmetic  7.94 us (3%)
    pallas_call x1, Pallas kernels, rest(): pl.pallas_call(partial(rest_body, (groups, shards), names), out_shape=[ja...  149 us
    pallas_call x1, Pallas kernels, exchange(): pl.pallas_call(partial(exchange_body, [(job[1], job[2]) for job in jobs],...  44.5 us
    unnamed x29, local copies, waits for them, and re-layouts  13 us
    pallas_call x1, Pallas kernels, attend(): pl.pallas_call(partial(attend_body, hpg, strength, ends.shape[0]), out_sh...  11.1 us

profile of v1, /device:TPU:0, one launch (start us, length us, event | category | flops | bytes accessed | tf_op | source)
XLA Modules:
  0.0 237.1 jit_solution(2025083365179786545)
XLA Ops:
  0.6 0.0 copy-start
  0.7 0.6 copy-done
  1.3 0.2 reduce-window.9
  1.5 1.3 broadcast_in_dim.18.refs_5_
  2.8 1.3 broadcast_in_dim.19.refs_6_
  4.0 1.3 broadcast_in_dim.17.refs_4_
  5.3 0.8 dynamic_slice.20
  6.1 0.6 broadcast_in_dim.16.refs_3_
  6.7 0.8 fusion.5
  7.5 1.2 constant_dynamic-slice_fusion
  8.7 0.0 copy-start.8
  8.7 0.0 copy-start.9
  8.7 0.9 concatenate.3.refs_1_
  9.6 44.5 %gather_start.1 = (bf16[8,128,768]{2,1,0:T(8,128)(2,1)}, bf16[4,192,704]{2,1,0:T(8,128)(2,1)}, bf16[4,192,768]{2,1,0:T(8,128)(2,1)}, bf16[4,192,768]{2,1,0:T(8,128)(2,1)}) custom-call(bf16[2,128,768]{2,1,0:T(8,128)(2,1)} %bitcast.35, bf16[192,704]{1,0:T(8,128)(2,1)} %concatenate.3.refs_1_, bf16[192,3072]{1,0:T(8,128)(2,1)} %refs_2_.1, bf16[192,768]{1,0:T(8,128)(2,1)} %refs_3_.1), custom_call_target="tpu_custom_call" | custom-call | tf_op jit(solution)/shard_map/gather_start/pallas_call | solution.py:425
  54.1 0.0 copy-start.5
  54.1 0.0 copy-start.6
  54.1 1.8 convert_reduce_fusion
  55.9 2.0 multiply_reduce_fusion
  57.9 0.0 copy-done.8
  57.9 0.0 copy-done.9
  58.0 0.0 copy-done.5
  58.0 0.6 add_convert_fusion.1
  58.6 0.0 copy-done.6
  58.6 1.4 convolution_convert_fusion.proj_ref.refs_13_
  60.0 0.0 copy-start.1
  60.0 2.4 fusion.1
  62.4 11.1 %attend.1 = (bf16[3,1024,1024]{2,1,0:T(8,128)(2,1)}, bf16[1024,1024]{1,0:T(8,128)(2,1)S(1)}, f32[1024,192]{1,0:T(8,128)S(1)}, f32[1024,3]{1,0:T(8,128)S(1)}) custom-call(s32[5]{0:T(128)S(1)} %bitcast.32, bf16[1024,704]{1,0:T(8,128)(2,1)S(1)} %convolution_convert_fusion.proj_ref.refs_13_), custom_call_target="tpu_custom_call" | custom-call | tf_op jit(solution)/shard_map/attend/pallas_call | solution.py:502
  73.5 0.0 copy-done.1
  73.5 0.0 copy-start.3
  73.5 1.3 copy-done.3
  74.8 0.0 copy-start.4
  74.8 0.8 copy-done.4
  75.6 0.0 copy-start.2
  75.6 0.9 convert_element_type.31
  76.6 0.2 copy-done.2
  76.8 148.6 %rest.1 = (bf16[256,768]{1,0:T(8,128)(2,1)}, bf16[256,768]{1,0:T(8,128)(2,1)}, f32[4,768]{1,0:T(4,128)}, f32[4,1,768]{2,1,0:T(1,128)}, f32[192,288]{1,0:T(8,128)...) custom-call(bf16[8,128,192]{2,1,0:T(8,128)(2,1)} %bitcast.33, bf16[256,768]{1,0:T(8,128)(2,1)} %bitcast.36, ...), custom_call_target="tpu_custom_call" | custom-call | tf_op jit(solution)/shard_map/rest/pallas_call | solution.py:1131
  225.5 0.0 copy-start.7
  225.5 0.0 copy-start.10
  225.5 1.5 slice_reduce_fusion
  227.0 1.9 copy.26
  228.8 1.8 copy.34
  230.6 1.8 copy.35
  232.4 1.7 copy.36
  234.1 1.5 copy.37
  235.6 0.0 copy-done.7
  235.6 0.7 copy.38
  236.3 0.0 copy-done.10
  236.3 0.6 copy.39
  (3 shorter events, 0.0 us)
Async XLA Ops:
  0.6 0.7 copy-start
  8.7 49.2 %copy-start.8 = (f32[768]{0:T(1024)S(1)}, f32[768]{0:T(1024)}, u32[]{:S(2)}) copy-start(f32[768]{0:T(1024)} %param.14) | copy-start | bytes 9220
  8.7 49.2 %copy-start.9 = (f32[768]{0:T(1024)S(1)}, f32[768]{0:T(1024)}, u32[]{:S(2)}) copy-start(f32[768]{0:T(1024)} %param.15) | copy-start | bytes 9220
  54.1 3.9 %copy-start.5 = (bf16[8,128,768]{2,1,0:T(8,128)(2,1)S(1)}, bf16[8,128,768]{2,1,0:T(8,128)(2,1)}, u32[]{:S(2)}) copy-start(bf16[8,128,768]{2,1,0:T(8,128)(2,1)} %get-tuple-element.27) | copy-start | bytes 4718596
  54.1 4.5 %copy-start.6 = (bf16[4,192,704]{2,1,0:T(8,128)(2,1)S(1)}, bf16[4,192,704]{2,1,0:T(8,128)(2,1)}, u32[]{:S(2)}) copy-start(bf16[4,192,704]{2,1,0:T(8,128)(2,1)} %get-tuple-element.28) | copy-start | bytes 3244036
  60.0 13.5 %copy-start.1 = (bf16[1024,704]{1,0:T(8,128)(2,1)}, bf16[1024,704]{1,0:T(8,128)(2,1)S(1)}, u32[]{:S(2)}) copy-start(bf16[1024,704]{1,0:T(8,128)(2,1)S(1)} %convolution_convert_fusion.proj_ref.refs_13_) | copy-start | bytes 4325380
  73.5 1.3 copy-start.3
  74.8 0.8 copy-start.4
  75.6 1.2 copy-start.2
  225.5 10.2 %copy-start.7 = (f32[192,384]{1,0:T(8,128)S(1)}, f32[192,384]{1,0:T(8,128)}, u32[]{:S(2)}) copy-start(f32[192,384]{1,0:T(8,128)} %get-tuple-element.88) | copy-start | bytes 884740
  225.5 10.9 %copy-start.10 = (f32[4,1,768]{2,1,0:T(1,128)S(1)}, f32[4,1,768]{2,1,0:T(1,128)}, u32[]{:S(2)}) copy-start(f32[4,1,768]{2,1,0:T(1,128)} %get-tuple-element.41) | copy-start | bytes 36868
